TPU v7x, 256 devices: a whole 4x4x8 slice. The times are simulated.
256 devices in a mesh: dp: 8 (over y, core), tm: 32 (over z, x).
Axes of the slice: x: 4, y: 4, z: 8, core: 2. Of those that a mesh axis runs over, the one named last changes fastest.
Arguments:
- frames: bfloat16 [65536, 1536], P(('dp', 'tm')), may hold values from -28 to 28, as said below
- seg: int32 [8, 8192], P('dp'), may hold values from 0 to 3, never falling along the last dimension, each value on 1 to 4096 neighbouring positions
- look_back: int32 [8, 32], P('dp'), may hold values 0 or 1
- w_dw: float32 [5, 1536], replicated, may hold values from -2.5 to 2.5
- w_qkv: bfloat16 [1536, 4608], P(None, 'dp'), may hold values from -0.15625 to 0.15625
- w_o: bfloat16 [1536, 1536], replicated, may hold values from -1.5 to 1.5
- cotangent: bfloat16 [65536, 1536], P(('dp', 'tm')), may hold values from -1 to 1
Outputs:
- mixed: bfloat16 [65536, 1536], P(('dp', 'tm'))
- weight_grad: float32 [1536, 1536], P('tm', 'dp')
Inputs may be any that keep to these rules, and one draw needn't show every extreme that they name: Float features; a few short runs of frames may be several times larger than the rest. `seg`: recording numbers never fall along a replica's frames; each recording has 1 to 4096 frames, one exactly 4096.
All inputs are finite; a program needn't handle non-finite values. No bound on the sum of `look_back` on one device may be relied on, other than what follows from the above.
Results may differ from a plain program's by a relative error of at most 0.012.
The roundings to bfloat16 on the way count: a program that leaves them out, or rounds other values in their place, can miss the bound.
Values may be sent and summed in bfloat16 or wider, within the bound.
A program may use at most 128 MiB of HBM per device.

v0:
```python
import math

import jax
import jax.numpy as jnp
from jax import lax
from jax.sharding import PartitionSpec as P

KER = 5
STRETCH = 256


def extended(block, sides, width):
    for axis, dim in sides:
        count = lax.axis_size(axis)
        forward = [(i, i + 1) for i in range(count - 1)]
        backward = [(target, source) for source, target in forward]
        low = lax.ppermute(
            lax.slice_in_dim(block, block.shape[dim] - width, None, axis=dim), axis, forward
        )
        high = lax.ppermute(lax.slice_in_dim(block, 0, width, axis=dim), axis, backward)
        block = jnp.concatenate([low, block, high], axis=dim)
    return block


def swapped(block, axis, distance):
    count = lax.axis_size(axis)
    route = []
    for low in range(count):
        high = low | 1 << distance
        if high != low and high < count:
            route += [(low, high), (high, low)]
    return lax.ppermute(block, axis, route)


def stretch_attention(queries, keys, values, seg_row, look_row, stretch):
    frame_count, heads_here, head_dim = queries.shape
    value_dim = values.shape[2]
    blocks = frame_count // stretch
    query_blocks = queries.reshape(blocks, stretch, heads_here, head_dim)
    key_blocks = keys.reshape(blocks, stretch, heads_here, head_dim)
    value_blocks = values.reshape(blocks, stretch, heads_here, value_dim)
    key_pairs = jnp.concatenate(
        [jnp.concatenate([jnp.zeros_like(key_blocks[:1]), key_blocks[:-1]], 0), key_blocks], 1
    )
    value_pairs = jnp.concatenate(
        [jnp.concatenate([jnp.zeros_like(value_blocks[:1]), value_blocks[:-1]], 0), value_blocks], 1
    )
    seg_blocks = seg_row.reshape(blocks, stretch)
    seg_pairs = jnp.concatenate(
        [jnp.concatenate([jnp.full((1, stretch), -1, jnp.int32), seg_blocks[:-1]], 0), seg_blocks],
        1,
    )
    allow_prev = look_row == 1
    per_step = math.gcd(blocks, max(1, 512 // stretch))
    current = jnp.arange(2 * stretch) >= stretch
    scale = 1.0 / math.sqrt(head_dim)

    def block_step(block_index):
        start = block_index * per_step

        def pick_rows(array):
            return lax.dynamic_slice_in_dim(array, start, per_step, 0)

        scores = (
            jnp.einsum(
                "gqhd,gkhd->ghqk",
                pick_rows(query_blocks),
                pick_rows(key_pairs),
                preferred_element_type=jnp.float32,
            )
            * scale
        )
        same_rec = pick_rows(seg_pairs)[:, None, :] == pick_rows(seg_blocks)[:, :, None]
        allowed = same_rec & (current[None, None, :] | pick_rows(allow_prev)[:, None, None])
        scores = jnp.where(allowed[:, None], scores, -1e30)
        row_max = jnp.max(scores, axis=-1, keepdims=True)
        raw_weights = jnp.exp(scores - row_max)
        probs = (raw_weights / jnp.sum(raw_weights, axis=-1, keepdims=True)).astype(jnp.bfloat16)
        outputs = jnp.einsum(
            "ghqk,gkhv->gqhv", probs, pick_rows(value_pairs), preferred_element_type=jnp.float32
        )
        return outputs.astype(jnp.bfloat16).reshape(per_step * stretch, heads_here * value_dim)

    mixed = lax.map(block_step, jnp.arange(blocks // per_step, dtype=jnp.int32))
    return mixed.reshape(frame_count, heads_here * value_dim)


def local(frames, seg, look_back, w_dw, w_qkv, w_o, cotangent):
    rows = frames.shape[0]
    width = frames.shape[1]
    tm_count = lax.axis_size("tm")
    piece = width // tm_count
    half = KER // 2
    padded = extended(frames, (("tm", 0),), half)
    seg_row = seg[0]
    look_row = look_back[0]
    seg_padded = jnp.pad(seg_row, (half, half), constant_values=-1)
    local_seg = lax.dynamic_slice_in_dim(
        seg_padded, lax.axis_index("tm") * rows, rows + 2 * half, 0
    )
    own_seg = local_seg[half : half + rows]
    total = jnp.zeros((rows, width), jnp.float32)
    for offset in range(KER):
        same_rec = (local_seg[offset : offset + rows] == own_seg).astype(jnp.float32)
        total = (
            total
            + w_dw[offset] * padded[offset : offset + rows].astype(jnp.float32) * same_rec[:, None]
        )
    activ = jax.nn.silu(total).astype(jnp.bfloat16)
    qkv = jnp.dot(
        activ, lax.all_gather(w_qkv, "dp", axis=1, tiled=True), preferred_element_type=jnp.float32
    ).astype(jnp.bfloat16)
    arranged = qkv.reshape(rows, 3, tm_count, piece)
    arrived = lax.all_to_all(arranged, "tm", split_axis=2, concat_axis=0, tiled=True)
    frame_count = arrived.shape[0]
    lower = lax.axis_index("tm") % 2 == 0
    own_pair = arrived[:, 0:2, 0, :]
    other_pair = swapped(own_pair, "tm", 0)
    joined = jnp.where(
        lower,
        jnp.concatenate([own_pair, other_pair], -1),
        jnp.concatenate([other_pair, own_pair], -1),
    )
    queries = joined[:, 0][:, None, :]
    keys = joined[:, 1][:, None, :]
    values = arrived[:, 2, 0, :][:, None, :]
    attended = stretch_attention(queries, keys, values, seg_row, look_row, STRETCH)
    returned = lax.all_to_all(
        attended.reshape(frame_count, 1, piece), "tm", split_axis=0, concat_axis=1, tiled=True
    )
    attn = returned.reshape(rows, width)
    mixed = jnp.dot(attn, w_o, preferred_element_type=jnp.float32).astype(jnp.bfloat16)
    grad_term = lax.dot_general(
        attn, cotangent, (((0,), (0,)), ((), ())), preferred_element_type=jnp.float32
    )
    row_share = lax.psum_scatter(grad_term, "tm", scatter_dimension=0, tiled=True)
    weight_grad = lax.psum_scatter(row_share, "dp", scatter_dimension=1, tiled=True)
    return (mixed, weight_grad)


def solution(mesh):
    placed = (
        P(("dp", "tm"), None),
        P("dp", None),
        P("dp", None),
        P(),
        P(None, "dp"),
        P(),
        P(("dp", "tm"), None),
    )
    return jax.shard_map(
        local,
        mesh=mesh,
        in_specs=placed,
        out_specs=(P(("dp", "tm"), None), P("tm", "dp")),
        check_vma=False,
    )
```

profile of v0, /device:TPU:97, one launch (start us, length us, event | category | flops | bytes accessed | tf_op | source)
XLA Modules:
  0.0 697.1 jit_solution(11983358287464709644)
XLA Ops:
  8.4 3.9 collective-permute-start.1
  12.3 1.9 collective-permute-start
  14.6 4.2 collective-permute-done
  18.8 69.9 %all-gather.2.cloned.1.call-done = bf16[1536,4608]{0,1:T(8,128)(2,1)} async-done(((bf16[1536,576]{0,1:T(8,128)(2,1)}), bf16[1536,4608]{0,1:T(8,128)(2,1)}) %all-gather.2.cloned.1.call-update) | async-done | bytes 14155792 | tf_op jit(solution)/shard_map/all_gather | solution.py:111
  88.7 11.5 %convolution_convert_fusion.1 = bf16[256,4608]{1,0:T(8,128)(2,1)} fusion(bf16[1536,4608]{0,1:T(8,128)(2,1)} %all-gather.2.cloned.1.call-done, bf16[256,1536]{1,0:T(8,128)(2,1)S(1)} %copy-done.4, bf16[2,1536]{1,0:T(2,128)(2,1)S(1)} %collective-permute-done, bf16[258,1536]{1,0:T(8,128)(2,1)S(1)} %constant_dynamic-update-slice_fusion.1, ...), kind=kOutput, calls=%fused_computation.23 | convolution fusion | flops 3636461568 | bytes 18925568 | tf_op jit(solution)/shard_map/dot_general | solution.py:110
  100.2 2.8 copy.24
  103.2 64.0 %all_to_all.33 = bf16[256,3,32,48]{0,3,1,2:T(8,128)(2,1)S(1)} all-to-all(bf16[256,3,32,48]{0,3,1,2:T(8,128)(2,1)S(1)} %copy.25), channel_id=1, replica_groups=mesh['dp'=8,'tm'=32] {'tm'}, dimensions={2} | all-to-all | bytes 4718592 | tf_op jit(solution)/shard_map/all_to_all | solution.py:114
  172.7 1.6 fusion.13
  174.3 28.8 %collective-permute-done.2 = bf16[8192,2,48]{0,2,1:T(8,128)(2,1)} collective-permute-done((bf16[8192,2,48]{0,2,1:T(8,128)(2,1)}, bf16[8192,2,48]{0,2,1:T(8,128)(2,1)}, u32[]{:S(2)}, u32[]{:S(2)}) %collective-permute-start.2) | collective-permute-done | bytes 1572896 | tf_op jit(solution)/shard_map/ppermute | solution.py:32
  203.1 3.8 maximum_select_fusion
  208.4 1.6 copy.44
  210.0 3.6 slice.109
  213.6 1.6 copy.43
  216.1 2.9 fusion.11
  218.9 98.1 %while.11 = (s32[]{:T(128)}, bf16[16,512,48]{1,2,0:T(8,128)(2,1)S(1)}, s32[16]{0:T(128)S(1)}, bf16[32,512,1,48]{1,0,3,2:T(8,128)(2,1)}, s32[32,512]{1,0:T(8,128)...) while((s32[]{:T(128)}, ...), condition=%wide.region_3.4_spmd.clone, body=%wide.region_0.3_spmd.clone.sunk | while | flops 77621248 | bytes 3646681 | solution.py:84
  226.3 1.3 constant_dynamic-slice_fusion.12
  232.4 1.3 constant_dynamic-slice_fusion.12
  238.6 1.3 constant_dynamic-slice_fusion.12
  244.7 1.3 constant_dynamic-slice_fusion.12
  317.9 2.0 copy.34
  319.9 6.2 reshape.89
  326.6 45.2 %reduce.20 = bf16[8192,48]{1,0:T(8,128)(2,1)S(1)} reduce(bf16[8192,1,48]{2,1,0:T(2,128)(2,1)} %reshape.89, bf16[]{:T(256)} %broadcast.84), dimensions={1}, to_apply=%reshape.89.reduce_sub_computation | reduce | bytes 1572866 | tf_op jit(solution)/shard_map/reshape;reshape | solution.py:129
  371.9 4.2 reshape.107
  376.1 26.1 %all_to_all.34 = bf16[32,2,6144]{2,1,0:T(2,128)(2,1)S(1)} all-to-all(bf16[32,2,6144]{2,1,0:T(2,128)(2,1)} %reshape.107), channel_id=1, replica_groups=mesh['dp'=8,'tm'=32] {'tm'}, dimensions={0} | all-to-all | bytes 1572864 | tf_op jit(solution)/shard_map/all_to_all | solution.py:128
  402.2 7.9 %reshape.108 = bf16[8192,1,48]{2,1,0:T(2,128)(2,1)} reshape(bf16[32,2,6144]{2,1,0:T(2,128)(2,1)S(1)} %all_to_all.34) | data formatting | bytes 1572864
  410.0 8.1 %copy.32 = bf16[8192,1,48]{0,2,1:T(8,128)(2,1)S(1)} copy(bf16[8192,1,48]{2,1,0:T(2,128)(2,1)} %reshape.108) | data formatting | bytes 1572864 | tf_op jit(solution)/shard_map/all_to_all | solution.py:128
  418.8 5.0 fusion.34
  423.9 227.7 %reduce-scatter.5.cloned.1.call-done = f32[48,1536]{1,0:T(8,128)} async-done(((f32[1536,1536]{1,0:T(8,128)}), f32[48,1536]{1,0:T(8,128)}) %reduce-scatter.5.cloned.1.call-update) | async-done | bytes 294928 | tf_op jit(solution)/shard_map/reduce_scatter | solution.py:136
  651.6 2.1 copy.35
  653.7 4.6 convolution_convert_fusion.2
  658.3 30.6 %reduce-scatter.7.cloned.1.call-done = f32[192,48]{1,0:T(8,128)} async-done(((f32[1536,48]{1,0:T(8,128)}), f32[192,48]{1,0:T(8,128)}) %reduce-scatter.7.cloned.1.call-update) | async-done | bytes 36880
  689.0 1.6 copy.36
  (275 shorter events, 92.5 us)
Async XLA Ops:
  7.2 411.6 %copy-start = (bf16[256,1536]{1,0:T(8,128)(2,1)S(1)}, bf16[256,1536]{1,0:T(8,128)(2,1)}, u32[]{:S(2)}) copy-start(bf16[256,1536]{1,0:T(8,128)(2,1)} %param.15) | copy-start | bytes 2359300
  7.2 1.2 copy-start.4
  7.2 7.1 %copy-start.7 = (s32[1,8192]{1,0:T(1,128)S(1)}, s32[1,8192]{1,0:T(1,128)}, u32[]{:S(2)}) copy-start(s32[1,8192]{1,0:T(1,128)} %param.10) | copy-start | bytes 98308
  7.2 7.3 %copy-start.8 = (f32[5,1536]{1,0:T(8,128)S(1)}, f32[5,1536]{1,0:T(8,128)}, u32[]{:S(2)}) copy-start(f32[5,1536]{1,0:T(8,128)} %param.12) | copy-start | bytes 92164
  7.2 81.5 %all-gather.2.cloned.1.call-start = ((), (), s32[]{:S(2)}) async-start(), calls=%async_computation.4 | async-start | bytes 15925248 | tf_op jit(solution)/shard_map/all_gather | solution.py:111
  7.9 643.6 %reduce-scatter.5.cloned.1.call-start = ((), (), s32[]{:S(2)}) async-start(), calls=%async_computation.5 | async-start | bytes 9732096 | tf_op jit(solution)/shard_map/reduce_scatter | solution.py:136
  8.4 6.2 collective-permute-start.1
  12.3 6.5 collective-permute-start
  167.5 2.6 copy-start.9
  168.8 34.3 %collective-permute-start.2 = (bf16[8192,2,48]{0,2,1:T(8,128)(2,1)}, bf16[8192,2,48]{0,2,1:T(8,128)(2,1)}, u32[]{:S(2)}, u32[]{:S(2)}) collective-permute-start(bf16[8192,2,48]{0,2,1:T(8,128)(2,1)} %slice_bitcast_fusion), channel_id=1, source_target_pairs={{0,1},{1,0},{2,3},{3,2},{4,5},{5,4},{6,7},{7,6},{8,9},{9,8},{10,11... | collective-permute-start | bytes 4718600 | tf_op jit(solution)/shard_map/ppermute | solution.py:32
  171.1 1.1 copy-start.3
  213.6 1.6 copy-start.1
  213.6 2.4 copy-start.2
  216.1 2.9 copy-start.5
  317.1 0.9 copy-start.6
  423.8 265.1 %reduce-scatter.7.cloned.1.call-start = ((), (), s32[]{:S(2)}) async-start(), calls=%async_computation.6 | async-start | bytes 884736
Sparse Core Ops, SparseCore 0:
  9.9 78.8 all-gather.1
  423.9 227.5 reduce-scatter.4
  654.1 34.7 reduce-scatter.6
where the time goes:
time: 704 us; the launch traced here: 697 us
  waiting for transfers between devices  362 us (51%)
  local copies, waits for them, and re-layouts  121 us (17%)
  blocking collectives  90.1 us (13%)
  other arithmetic  55.5 us (8%)
  matrix products  36.9 us (5%)
  between operations  14 us (2%)
  loops' own time  11.7 us (2%)
    reduce_scatter x1, waiting for transfers between devices, local(): lax.psum_scatter(grad_term, 'tm', scatter_dimension=0, tiled=True)  228 us
    all_gather x1, waiting for transfers between devices, local(): lax.all_gather(w_qkv, 'dp', axis=1, tiled=True)  69.9 us
    all_to_all x1, blocking collectives, local(): lax.all_to_all(arranged, 'tm', split_axis=2, concat_axis=0, tiled=True)  64 us
    dynamic_slice x96, local copies, waits for them, and re-layouts, pick_rows(): return lax.dynamic_slice_in_dim(array, start, per_step, 0)  58.5 us
    another operation x1, other arithmetic, local(): attended.reshape(frame_count, 1, piece)  45.2 us
    unnamed x4, waiting for transfers between devices  31.3 us
    ppermute x1, waiting for transfers between devices, swapped(): return lax.ppermute(block, axis, route)  28.8 us
    all_to_all x1, blocking collectives, local(): lax.all_to_all(attended.reshape(frame_count, 1, piece), 'tm', split_axis=...  26.1 us
  transfers between devices with their start and end apart: 6, of which 5 were waited for; matrix products, arithmetic and copies ran while one was open for 1% of the time, Pallas kernels for 0%

commit v1 on v0

v1 whole, which is shorter than its diff:
```python
import math

import jax
import jax.numpy as jnp
from jax import lax
from jax.sharding import PartitionSpec as P

KER = 5
HEADS = 16
HALF = KER // 2


def conv_silu(rows_in, seg_in, w_dw):
    count = rows_in.shape[0] - 2 * HALF
    own = seg_in[HALF : HALF + count]
    total = jnp.zeros((count, rows_in.shape[1]), jnp.float32)
    for offset in range(KER):
        same = (seg_in[offset : offset + count] == own).astype(jnp.float32)
        total = total + w_dw[offset] * rows_in[offset : offset + count].astype(jnp.float32) * same[:, None]
    return jax.nn.silu(total).astype(jnp.bfloat16)


def local(frames, seg, look_back, w_dw, w_qkv, w_o, cotangent):
    rows, width = frames.shape
    count = lax.axis_size("tm")
    me = lax.axis_index("tm")
    weights = lax.all_gather(w_qkv, "dp", axis=1, tiled=True)
    before = lax.ppermute(frames, "tm", [(i, i + 1) for i in range(count - 1)])
    far = lax.ppermute(frames[-HALF:], "tm", [(i, i + 2) for i in range(count - 2)])
    after = lax.ppermute(frames[:HALF], "tm", [(i + 1, i) for i in range(count - 1)])
    stack = jnp.concatenate([far, before, frames, after], 0)
    seg_padded = jnp.pad(seg[0], (rows + HALF, HALF), constant_values=-1)
    local_seg = lax.dynamic_slice_in_dim(seg_padded, me * rows, 2 * rows + 2 * HALF, 0)
    activ = conv_silu(stack, local_seg, w_dw)
    qkv = jnp.dot(activ[rows:], weights, preferred_element_type=jnp.float32).astype(jnp.bfloat16)
    kv_before = jnp.dot(
        activ[:rows], weights[:, width:], preferred_element_type=jnp.float32
    ).astype(jnp.bfloat16)
    head_dim = width // HEADS
    queries = qkv[:, :width].reshape(rows, HEADS, head_dim)
    kv = jnp.concatenate([kv_before, qkv[:, width:]], 0).reshape(2 * rows, 2, HEADS, head_dim)
    scores = jnp.einsum(
        "qhd,khd->hqk", queries, kv[:, 0], preferred_element_type=jnp.float32
    ) * (1.0 / math.sqrt(head_dim))
    seg_pair = local_seg[HALF : HALF + 2 * rows]
    same_rec = seg_pair[rows:][:, None] == seg_pair[None, :]
    look = lax.dynamic_slice_in_dim(look_back[0], me, 1, 0)[0] == 1
    allowed = same_rec & ((jnp.arange(2 * rows) >= rows) | look)[None, :]
    scores = jnp.where(allowed[None], scores, -1e30)
    raw = jnp.exp(scores - jnp.max(scores, axis=-1, keepdims=True))
    probs = (raw / jnp.sum(raw, axis=-1, keepdims=True)).astype(jnp.bfloat16)
    attn = jnp.einsum("hqk,khv->qhv", probs, kv[:, 1], preferred_element_type=jnp.float32)
    attn = attn.astype(jnp.bfloat16).reshape(rows, width)
    mixed = jnp.dot(attn, w_o, preferred_element_type=jnp.float32).astype(jnp.bfloat16)
    grad_term = lax.dot_general(
        attn, cotangent, (((0,), (0,)), ((), ())), preferred_element_type=jnp.float32
    )
    col_share = lax.psum_scatter(grad_term, "dp", scatter_dimension=1, tiled=True)
    weight_grad = lax.psum_scatter(col_share, "tm", scatter_dimension=0, tiled=True)
    return (mixed, weight_grad)


def solution(mesh):
    placed = (
        P(("dp", "tm"), None),
        P("dp", None),
        P("dp", None),
        P(),
        P(None, "dp"),
        P(),
        P(("dp", "tm"), None),
    )
    return jax.shard_map(
        local,
        mesh=mesh,
        in_specs=placed,
        out_specs=(P(("dp", "tm"), None), P("tm", "dp")),
        check_vma=False,
    )
```

time: 704 us -> 420 us (0.60)
  local copies, waits for them, and re-layouts: 121 us -> 13.2 us
  blocking collectives: 90.1 us -> 0 us
  other arithmetic: 55.5 us -> 15.8 us
  waiting for transfers between devices: 362 us -> 324 us
  loops' own time: 11.7 us -> 0 us
    unnamed x4, waiting for transfers between devices: 31.3 us -> 207 us
    reduce_scatter x1, waiting for transfers between devices: 228 us -> 59.6 us  [local(): lax.psum_scatter(grad_term, 'dp', scatter_dimension=1, tiled=True)]
    all_to_all x2 -> x0, blocking collectives: 90.1 us -> none  [the longest x1 64 us: local(): lax.all_to_all(arranged, 'tm', split_axis=2, concat_axis=0, tiled=True)]
    dynamic_slice x113 -> x1, local copies, waits for them, and re-layouts: 68 us -> 0.79 us  [local(): lax.dynamic_slice_in_dim(seg_padded, me * rows, 2 * rows + 2 * HALF, 0)]
    another operation x1 -> x0, other arithmetic: 45.2 us -> none  [local(): attended.reshape(frame_count, 1, piece)]
    ppermute x3, waiting for transfers between devices: 33 us -> 6.26 us  [the longest x1 6.25 us: local(): before = lax.ppermute(frames, 'tm', [(i, i + 1) for i in range(count - 1)])]
    unnamed x30 -> x13, local copies, waits for them, and re-layouts: 22.9 us -> 5.07 us
    all_gather x1, waiting for transfers between devices: 69.9 us -> 52.1 us  [local(): weights = lax.all_gather(w_qkv, 'dp', axis=1, tiled=True)]
  transfers between devices with their start and end apart: 6 -> 6, of which waited for: 5 -> 4; matrix products, arithmetic and copies ran while one was open for 1% -> 4% of each run, Pallas kernels for 0% -> 0%
where the time goes in v1:
time: 420 us; the launch traced here: 412 us
  waiting for transfers between devices  324 us (77%)
  matrix products  32.8 us (8%)
  other arithmetic  15.8 us (4%)
  between operations  13.9 us (3%)
  local copies, waits for them, and re-layouts  13.2 us (3%)
  starting transfers between devices  11.6 us (3%)
    unnamed x4, waiting for transfers between devices  207 us
    reduce_scatter x1, waiting for transfers between devices, local(): lax.psum_scatter(grad_term, 'dp', scatter_dimension=1, tiled=True)  59.6 us
    all_gather x1, waiting for transfers between devices, local(): weights = lax.all_gather(w_qkv, 'dp', axis=1, tiled=True)  52.1 us
    dot_general x1, matrix products, local(): jnp.dot(activ[rows:], weights, preferred_element_type=jnp.float32)  9.13 us
  transfers between devices with their start and end apart: 6, of which 4 were waited for; matrix products, arithmetic and copies ran while one was open for 4% of the time, Pallas kernels for 0%

profile of v1, /device:TPU:97, one launch (start us, length us, event | category | flops | bytes accessed | tf_op | source)
XLA Modules:
  0.0 411.7 jit_solution(788652810859067581)
XLA Ops:
  7.2 0.7 all-gather.2.cloned.1.call-update
  8.0 3.1 collective-permute-start.1
  11.1 0.8 fusion.22
  11.9 4.4 %collective-permute-start = (bf16[2,1536]{1,0:T(2,128)(2,1)S(1)}, bf16[2,1536]{1,0:T(2,128)(2,1)S(1)}, u32[]{:S(2)}, u32[]{:S(2)}) collective-permute-start(bf16[2,1536]{1,0:T(2,128)(2,1)S(1)} %get-tuple-element.13), channel_id=1, source_target_pairs={{0,2},{1,3},{2,4},{3,5},{4,6},{5,7},{6,8},{7,9},{8,10},{9,11},{10,... | collective-permute-start | bytes 18440 | tf_op jit(solution)/shard_map/ppermute | solution.py:29
  16.3 4.0 collective-permute-start.2
  20.2 0.8 pad_dynamic-slice_fusion
  21.0 0.1 slice.102
  21.1 0.1 slice.85
  21.2 1.2 fusion.23
  22.4 0.7 fusion.19
  23.1 1.1 slice_reduce_fusion.4
  24.2 0.1 fusion.15
  24.3 0.2 compare_and_fusion
  24.4 6.3 %collective-permute-done.1 = bf16[256,1536]{1,0:T(8,128)(2,1)S(1)} collective-permute-done((bf16[256,1536]{1,0:T(8,128)(2,1)}, bf16[256,1536]{1,0:T(8,128)(2,1)S(1)}, u32[]{:S(2)}, u32[]{:S(2)}) %collective-permute-start.1) | collective-permute-done | bytes 786464 | tf_op jit(solution)/shard_map/ppermute | solution.py:28
  30.8 0.4 pad_maximum_fusion.1
  31.2 5.4 %multiply_convert_fusion = bf16[512,1536]{1,0:T(8,128)(2,1)} fusion(bf16[514,1536]{1,0:T(8,128)(2,1)S(1)} %constant_dynamic-update-slice_fusion, bf16[514,1536]{1,0:T(8,128)(2,1)S(1)} %pad_maximum_fusion.1, bf16[256,1536]{1,0:T(8,128)(2,1)S(1)} %copy-done.1, bf16[256,1536]{1,0:T(8,128)(2,1)S(1)} %collective-permute-done.1, f32[512]{0:T(512)S(1)} %get-tuple-element.16, ...), kind=kLoop, calls=%fused_computation.14 | loop fusion | flops 20447232 | bytes 9476096 | tf_op jit(solution)/shard_map/convert_element_type | solution.py:20
  36.6 52.1 %all-gather.2.cloned.1.call-done = bf16[1536,4608]{0,1:T(8,128)(2,1)} async-done(((bf16[1536,576]{0,1:T(8,128)(2,1)}), bf16[1536,4608]{0,1:T(8,128)(2,1)}) %all-gather.2.cloned.1.call-update) | async-done | bytes 14155792 | tf_op jit(solution)/shard_map/all_gather | solution.py:27
  88.7 9.1 %convolution_convert_fusion = bf16[256,4608]{1,0:T(8,128)(2,1)S(1)} fusion(bf16[1536,4608]{0,1:T(8,128)(2,1)} %all-gather.2.cloned.1.call-done, bf16[512,1536]{1,0:T(8,128)(2,1)} %multiply_convert_fusion), kind=kOutput, calls=%fused_computation.6 | convolution fusion | flops 3625058304 | bytes 17301504 | tf_op jit(solution)/shard_map/dot_general | solution.py:35
  97.9 0.2 slice.112
  98.1 2.0 copy-done.4
  100.1 6.4 %fusion.8 = bf16[256,3072]{1,0:T(8,128)(2,1)S(1)} fusion(bf16[1536,4608]{0,1:T(8,128)(2,1)} %all-gather.2.cloned.1.call-done, bf16[512,1536]{1,0:T(8,128)(2,1)S(1)} %copy-done.4), kind=kOutput, calls=%fused_computation.12 | convolution fusion | flops 2416705536 | bytes 11796480 | tf_op jit(solution)/shard_map/dot_general | solution.py:36
  106.5 1.9 pad_maximum_fusion
  108.4 4.8 %copy.16 = bf16[512,3072]{0,1:T(8,128)(2,1)} copy(bf16[512,3072]{1,0:T(8,128)(2,1)} %pad_maximum_fusion) | data formatting | bytes 6291456 | tf_op jit(solution)/shard_map/concatenate | solution.py:41
  113.2 0.3 copy.17
  113.5 2.7 fusion.11
  116.2 6.0 %fusion.24 = (f32[16,256]{1,0:T(8,128)S(1)}, f32[16,256,512]{2,1,0:T(8,128)}) fusion(f32[16,256,512]{2,1,0:T(8,128)S(1)} %fusion.11, pred[256,512]{1,0:T(8,128)(4,1)S(1)} %compare_and_fusion), kind=kOutput, calls=%fused_computation.48 | output fusion | flops 12583423 | bytes 16924672 | tf_op jit(solution)/shard_map/sub | solution.py:50
  122.2 4.9 %fusion.12 = bf16[16,96,256]{2,1,0:T(8,128)(2,1)S(1)} fusion(f32[16,256,512]{2,1,0:T(8,128)} %get-tuple-element.20, f32[16,256]{1,0:T(8,128)S(1)} %get-tuple-element.19, bf16[512,2,16,96]{0,3,2,1:T(8,128)(2,1)S(1)} %bitcast.23), kind=kOutput, calls=%fused_computation.20 | convolution fusion | flops 407240704 | bytes 10764288 | tf_op jit(solution)/shard_map/hqk,khv->qhv/dot_general | solution.py:52
  127.1 5.1 %fusion.25 = f32[1536,1536]{0,1:T(8,128)} fusion(bf16[256,1536]{0,1:T(8,128)(2,1)S(1)} %bitcast.25, bf16[256,1536]{1,0:T(8,128)(2,1)S(1)} %copy-done), kind=kOutput, calls=%fused_computation.49 | convolution fusion | flops 1207959552 | bytes 11010048 | tf_op jit(solution)/shard_map/dot_general | solution.py:55
  132.3 59.6 %reduce-scatter.5.cloned.1.call-done = f32[1536,192]{0,1:T(8,128)} async-done(((f32[1536,1536]{0,1:T(8,128)}), f32[1536,192]{0,1:T(8,128)}) %reduce-scatter.5.cloned.1.call-update) | async-done | bytes 1179664 | tf_op jit(solution)/shard_map/reduce_scatter | solution.py:58
  191.9 2.9 copy.19
  194.8 4.6 %convolution_convert_fusion.1 = bf16[256,1536]{1,0:T(8,128)(2,1)} fusion(bf16[256,1536]{0,1:T(8,128)(2,1)S(1)} %bitcast.26, bf16[1536,1536]{1,0:T(8,128)(2,1)} %param.12), kind=kOutput, calls=%fused_computation.15 | convolution fusion | flops 1208352768 | bytes 6291456 | tf_op jit(solution)/shard_map/dot_general | solution.py:54
  199.4 205.8 %reduce-scatter.7.cloned.1.call-done = f32[48,192]{1,0:T(8,128)} async-done(((f32[1536,192]{1,0:T(8,128)}), f32[48,192]{1,0:T(8,128)}) %reduce-scatter.7.cloned.1.call-update) | async-done | bytes 36880
  (21 shorter events, 0.3 us)
Async XLA Ops:
  7.2 120.0 %copy-start = (bf16[256,1536]{1,0:T(8,128)(2,1)S(1)}, bf16[256,1536]{1,0:T(8,128)(2,1)}, u32[]{:S(2)}) copy-start(bf16[256,1536]{1,0:T(8,128)(2,1)} %param.13) | copy-start | bytes 2359300
  7.2 23.5 %copy-start.1 = (bf16[256,1536]{1,0:T(8,128)(2,1)S(1)}, bf16[256,1536]{1,0:T(8,128)(2,1)}, u32[]{:S(2)}) copy-start(bf16[256,1536]{1,0:T(8,128)(2,1)} %param.7) | copy-start | bytes 2359300
  7.2 81.5 %all-gather.2.cloned.1.call-start = ((), (), s32[]{:S(2)}) async-start(), calls=%async_computation.2 | async-start | bytes 15925248 | tf_op jit(solution)/shard_map/all_gather | solution.py:27
  7.9 183.9 %reduce-scatter.5.cloned.1.call-start = ((), (), s32[]{:S(2)}) async-start(), calls=%async_computation.3 | async-start | bytes 10616832 | tf_op jit(solution)/shard_map/reduce_scatter | solution.py:58
  8.0 22.7 %collective-permute-start.1 = (bf16[256,1536]{1,0:T(8,128)(2,1)}, bf16[256,1536]{1,0:T(8,128)(2,1)S(1)}, u32[]{:S(2)}, u32[]{:S(2)}) collective-permute-start(bf16[256,1536]{1,0:T(8,128)(2,1)} %param.7), channel_id=1, source_target_pairs={{0,1},{1,2},{2,3},{3,4},{4,5},{5,6},{6,7},{7,8},{8,9},{9,10},{10,1... | collective-permute-start | bytes 2359304 | tf_op jit(solution)/shard_map/ppermute | solution.py:28
  11.9 18.9 %collective-permute-start = (bf16[2,1536]{1,0:T(2,128)(2,1)S(1)}, bf16[2,1536]{1,0:T(2,128)(2,1)S(1)}, u32[]{:S(2)}, u32[]{:S(2)}) collective-permute-start(bf16[2,1536]{1,0:T(2,128)(2,1)S(1)} %get-tuple-element.13), channel_id=1, source_target_pairs={{0,2},{1,3},{2,4},{3,5},{4,6},{5,7},{6,8},{7,9},{8,10},{9,11},{10,... | collective-permute-start | bytes 18440 | tf_op jit(solution)/shard_map/ppermute | solution.py:29
  16.3 14.5 %collective-permute-start.2 = (bf16[2,1536]{1,0:T(2,128)(2,1)S(1)}, bf16[2,1536]{1,0:T(2,128)(2,1)S(1)}, u32[]{:S(2)}, u32[]{:S(2)}) collective-permute-start(bf16[2,1536]{1,0:T(2,128)(2,1)S(1)} %get-tuple-element.14), channel_id=1, source_target_pairs={{1,0},{2,1},{3,2},{4,3},{5,4},{6,5},{7,6},{8,7},{9,8},{10,9},{11,1... | collective-permute-start | bytes 18440 | tf_op jit(solution)/shard_map/ppermute | solution.py:30
  97.9 8.7 %copy-start.3 = (bf16[256,4608]{1,0:T(8,128)(2,1)}, bf16[256,4608]{1,0:T(8,128)(2,1)S(1)}, u32[]{:S(2)}) copy-start(bf16[256,4608]{1,0:T(8,128)(2,1)S(1)} %convolution_convert_fusion) | copy-start | bytes 7077892
  97.9 2.3 copy-start.4
  108.4 4.8 %slice-start = ((bf16[256,4608]{1,0:T(8,128)(2,1)}), bf16[256,1536]{1,0:T(8,128)(2,1)S(1)}, s32[]{:S(2)}) async-start(bf16[256,4608]{1,0:T(8,128)(2,1)} %copy-done.3), calls=%async_computation.5 | async-start | bytes 1572864 | tf_op jit(solution)/shard_map/slice | solution.py:40
  116.2 6.0 %copy-start.2 = (bf16[512,3072]{0,1:T(8,128)(2,1)S(1)}, bf16[512,3072]{0,1:T(8,128)(2,1)}, u32[]{:S(2)}) copy-start(bf16[512,3072]{0,1:T(8,128)(2,1)} %copy.16) | copy-start | bytes 9437188
  132.2 273.0 %reduce-scatter.7.cloned.1.call-start = ((), (), s32[]{:S(2)}) async-start(), calls=%async_computation.4 | async-start | bytes 1622016
Sparse Core Ops, SparseCore 0:
  9.9 78.8 all-gather.1
  132.3 59.4 reduce-scatter.4
  196.3 208.8 reduce-scatter.6

commit v2 on v1

v2 whole, which is shorter than its diff:
```python
import functools
import math

import jax
import jax.numpy as jnp
from jax import lax
from jax.experimental import pallas as pl
from jax.experimental.pallas import tpu as pltpu
from jax.sharding import PartitionSpec as P

MESH = pl.DeviceIdType.MESH
BF = jnp.bfloat16
F32 = jnp.float32

KER = 5
HALF = 2
ROWS = 256
WIDTH = 1536
HDIM = 96
UNIT = 192
QUARTER = 48
PAIRS = 4
NX, NY, NZ = 4, 4, 8
COLS = 384
EDGE = 16
CHUNK = 64
NT = (((1,), (1,)), ((), ()))
DIRECT = 1


def dot(a, b):
    return jnp.dot(a, b, preferred_element_type=F32)


def dot_nt(a, b):
    return lax.dot_general(a, b, NT, preferred_element_type=F32)


def wait_for(ref, sem):
    pltpu.make_async_copy(ref, ref, sem).wait()


def identity(n):
    return (
        lax.broadcasted_iota(jnp.int32, (n, n), 0) == lax.broadcasted_iota(jnp.int32, (n, n), 1)
    ).astype(BF)


def kernel(
    frames, cmask, lohi, w_dw, w_qkv, cot, w_o, mixed, wgrad,
    wt, units, ext, halo, mask_b, acts, lohi_b, w_o_v, cot_sib, q_t, k_n, v_t, at, at_sib,
    gf, gb, r1, s1f, s1b, r2, s2b, r3,
    w_send, w_recv, f_send, halo_send, halo_recv, act_send, act_recv, small_send, small_recv,
    at_send, at_recv, g1_send, g1_recv, g2_send, g2_recv, g3_send, g3_recv, wo_sem,
):
    dp, tm = lax.axis_index("dp"), lax.axis_index("tm")
    y, c = lax.div(dp, 2), lax.rem(dp, 2)
    z, x = lax.div(tm, 4), lax.rem(tm, 4)
    oc = 1 - c

    def dev(yy, cc, zz, xx):
        return {"dp": yy * 2 + cc, "tm": zz * 4 + xx}

    def plus(v, d, n):
        return lax.rem(v + d, n)

    def rcopy(src, dst, send, recv, device):
        return pltpu.make_async_remote_copy(
            src_ref=src, dst_ref=dst, send_sem=send, recv_sem=recv,
            device_id=device, device_id_type=MESH,
        )

    sibling = dev(y, oc, z, x)
    following = {"dp": dp, "tm": plus(tm, 1, 32)}
    preceding = {"dp": dp, "tm": plus(tm, 31, 32)}
    x_low = dev(y, c, z, plus(x, NX - 1, NX))

    partners = [sibling, following, preceding]
    for d in range(1, NY):
        partners += [dev(plus(y, d, NY), c, z, x), dev(plus(y, d, NY), oc, z, x)]
    for d in range(1, NX):
        partners += [dev(y, c, z, plus(x, d, NX))]
    for d in range(1, NZ):
        partners += [dev(y, c, plus(z, d, NZ), x), dev(y, oc, plus(z, d, NZ), x)]
    barrier = pltpu.get_barrier_semaphore()
    for device in partners:
        pl.semaphore_signal(barrier, inc=1, device_id=device, device_id_type=MESH)

    wo_copy = pltpu.make_async_copy(w_o, w_o_v, wo_sem)
    wo_copy.start()
    eye = identity(3 * UNIT)

    def turn(i, _):
        part = pl.ds(pl.multiple_of(i * 256, 256), 256)
        turned = dot_nt(eye, w_qkv[part, :]).astype(BF)
        for j in range(3):
            wt[j, :, part] = turned[j * UNIT : (j + 1) * UNIT]
        return 0

    lax.fori_loop(0, WIDTH // 256, turn, 0)
    for o in range(KER):
        mask_b[o] = jnp.broadcast_to(cmask[:, o : o + 1], (ROWS, 128))
    ext[EDGE : EDGE + ROWS] = frames[...].astype(F32)
    lohi_b[c] = lohi[...]

    pl.semaphore_wait(barrier, len(partners))

    up = rcopy(frames.at[ROWS - EDGE : ROWS], halo.at[0], halo_send.at[0], halo_recv.at[0], following)
    down = rcopy(frames.at[0:EDGE], halo.at[1], halo_send.at[1], halo_recv.at[1], preceding)
    up.start()
    down.start()
    lohi_copy = rcopy(lohi, lohi_b.at[c], small_send.at[0], small_recv.at[0], sibling)
    lohi_copy.start()

    mine = lax.rem(x, 2) + 2 * lax.rem(z, 2)
    from_x = (1 - lax.rem(x, 2)) + 2 * lax.rem(z, 2)
    from_z = lax.rem(x, 2) + 2 * (1 - lax.rem(z, 2))
    from_xz = (1 - lax.rem(x, 2)) + 2 * (1 - lax.rem(z, 2))
    first = lax.rem(3 * dp, 4)
    offset = jnp.where(first == 3, 1, jnp.where(first == 2, 2, 0))

    def owned(jj):
        j = lax.rem(jj + offset, 3)
        u = 3 * dp + j
        return j, lax.rem(u, 4) * 3 + lax.div(u, 8), lax.rem(lax.div(u, 4), 2)

    def to_y(jj, d, e):
        j, idx, core = owned(jj)
        part = lax.rem(mine + e, 4)
        return rcopy(
            wt.at[j, pl.ds(pl.multiple_of(part * QUARTER, QUARTER), QUARTER)],
            units.at[idx, part], w_send.at[jj, d, e], w_recv.at[idx, part],
            dev(plus(y, d, NY), core, z, x),
        )

    def to_sibling(jj, e):
        j, idx, core = owned(jj)
        return rcopy(
            wt.at[j, e * QUARTER : (e + 1) * QUARTER],
            units.at[idx, e], w_send.at[jj, 0, e], w_recv.at[idx, e], sibling,
        )

    def send_own(jj, _):
        j, idx, core = owned(jj)
        for d in (1, 3, 2):
            to_y(jj, d, 0).start()

        @pl.when(idx < DIRECT)
        def _():
            for e in range(1, 4):
                for d in (1, 3, 2):
                    to_y(jj, d, e).start()

        @pl.when(core != c)
        def _():
            for e in range(4):
                to_sibling(jj, e).start()

        @pl.when(core == c)
        def _():
            for e in range(4):
                pltpu.make_async_copy(
                    wt.at[j, e * QUARTER : (e + 1) * QUARTER], units.at[idx, e], w_recv.at[idx, e]
                ).start()

        return 0

    lax.fori_loop(0, 3, send_own, 0)

    wait_for(halo.at[0], halo_recv.at[0])
    wait_for(halo.at[1], halo_recv.at[1])
    ext[0:EDGE] = halo[0].astype(F32)
    ext[EDGE + ROWS :] = halo[1].astype(F32)

    def act_copy(i, r):
        rows = pl.ds(r * CHUNK, CHUNK)
        device, place = ((sibling, 2 * c + 1), (following, 2 * c))[i]
        return rcopy(
            acts.at[2 * c + 1, rows], acts.at[place, rows], act_send.at[i, r], act_recv.at[i, r], device
        )

    def act_pass(r):
        rows = pl.ds(r * CHUNK, CHUNK)
        return rcopy(
            acts.at[2 * c, rows], acts.at[2 * c, rows], act_send.at[2, r], act_recv.at[2, r], sibling
        )

    for r in range(ROWS // CHUNK):

        def column(i, _, r=r):
            lanes = pl.ds(pl.multiple_of(i * 128, 128), 128)
            total = jnp.zeros((CHUNK, 128), F32)
            for o in range(KER):
                window = ext[EDGE - HALF + r * CHUNK + o : EDGE - HALF + r * CHUNK + o + CHUNK, lanes]
                total = total + w_dw[o : o + 1, lanes] * window * mask_b[o, r * CHUNK : (r + 1) * CHUNK]
            acts[2 * c + 1, r * CHUNK : (r + 1) * CHUNK, lanes] = (total / (1.0 + jnp.exp(-total))).astype(BF)
            return 0

        lax.fori_loop(0, WIDTH // 128, column, 0)
        act_copy(1, r).start()
        act_copy(0, r).start()

    cot_copy = rcopy(cot, cot_sib, small_send.at[1], small_recv.at[1], sibling)
    cot_copy.start()

    def foreign(hp, t):
        u = 8 * t + 4 * c + hp
        idx = hp * 3 + t
        return idx, (lax.div(u, 6) != y) & (idx >= DIRECT)

    def along_z(idx):
        step = jnp.where(lax.rem(idx, 2) == 0, 1, NZ - 1)
        return dev(y, c, plus(z, step, NZ), x)

    def pass_copy(idx, i):
        part = (mine, mine, from_x)[i]
        device = (x_low, along_z(idx), along_z(idx))[i]
        return rcopy(units.at[idx, part], units.at[idx, part], f_send.at[idx, i], w_recv.at[idx, part], device)

    def pump_first(hp):
        for t in range(3):
            idx, need = foreign(hp, t)

            @pl.when(need)
            def _(idx=idx):
                wait_for(units.at[idx, mine], w_recv.at[idx, mine])
                pass_copy(idx, 0).start()
                pass_copy(idx, 1).start()

    def pump_second(hp):
        for t in range(3):
            idx, need = foreign(hp, t)

            @pl.when(need)
            def _(idx=idx):
                wait_for(units.at[idx, from_x], w_recv.at[idx, from_x])
                pass_copy(idx, 2).start()

    def wait_unit(hp, t):
        idx, need = foreign(hp, t)

        @pl.when(need)
        def _():
            wait_for(units.at[idx, from_z], w_recv.at[idx, from_z])
            wait_for(units.at[idx, from_xz], w_recv.at[idx, from_xz])

        @pl.when(jnp.logical_not(need))
        def _():
            for e in range(4):
                wait_for(units.at[idx, e], w_recv.at[idx, e])

    def unit(hp, t):
        return units[hp * 3 + t].reshape(UNIT, WIDTH)

    def keys_values(hp, part):
        where = slice(part * ROWS, (part + 1) * ROWS)
        for s in range(2):
            k_n[hp, s, where] = dot_nt(acts[2 * s + part], unit(hp, 1)).astype(BF)
            v_t[hp, s, :, where] = dot_nt(unit(hp, 2), acts[2 * s + part]).astype(BF)

    def own_part(hp):
        for t in range(3):
            wait_unit(hp, t)
        for s in range(2):
            q_t[hp, s] = dot_nt(unit(hp, 0), acts[2 * s + 1]).astype(BF)
        keys_values(hp, 1)

    def advance(g, _):
        pl.when(g < PAIRS)(lambda: pump_first(g))
        pl.when((g >= 1) & (g <= PAIRS))(lambda: pump_second(g - 1))

        @pl.when(g == 2)
        def _():
            for r in range(ROWS // CHUNK):
                rows = pl.ds(r * CHUNK, CHUNK)
                wait_for(acts.at[2 * oc + 1, rows], act_recv.at[0, r])

        pl.when(g >= 2)(lambda: own_part(g - 2))

        @pl.when(g == PAIRS)
        def _():
            for r in range(ROWS // CHUNK):
                rows = pl.ds(r * CHUNK, CHUNK)
                wait_for(acts.at[2 * c, rows], act_recv.at[1, r])
                act_pass(r).start()

        return 0

    lax.fori_loop(0, PAIRS + 2, advance, 0)

    for r in range(ROWS // CHUNK):
        rows = pl.ds(r * CHUNK, CHUNK)
        wait_for(acts.at[2 * oc, rows], act_recv.at[2, r])
    wait_for(lohi_b.at[oc], small_recv.at[0])
    wait_for(cot_sib, small_recv.at[1])

    factor = math.log2(math.e) / math.sqrt(HDIM)

    def attend(hp):
        def one(s, _):
            q = q_t[hp, s]
            zero = jnp.zeros((HDIM, ROWS), BF)
            both = jnp.concatenate(
                [jnp.concatenate([q[:HDIM], zero], 0), jnp.concatenate([zero, q[HDIM:]], 0)], 1
            )
            scores = dot(k_n[hp, s], both)
            bounds = lohi_b[s]
            at_j = lax.broadcasted_iota(jnp.int32, (2 * ROWS, ROWS), 0)
            allowed = (at_j >= bounds[0:1]) & (at_j < bounds[1:2])
            for e in range(2):
                mine_scores = jnp.where(allowed, scores[:, e * ROWS : (e + 1) * ROWS], -1e30)
                top = jnp.max(mine_scores, axis=0, keepdims=True)
                raw = jnp.exp2((mine_scores - top) * factor)
                probs = (raw * (1.0 / jnp.sum(raw, axis=0, keepdims=True))).astype(BF)
                at[hp, s, e * HDIM : (e + 1) * HDIM] = dot(
                    v_t[hp, s, e * HDIM : (e + 1) * HDIM], probs
                ).astype(BF)
            return 0

        lax.fori_loop(0, 2, one, 0)

    def at_copy(hp):
        return rcopy(at.at[hp, oc], at_sib.at[hp], at_send.at[hp], at_recv.at[hp], sibling)

    def grad(hp):
        for v in range(NY):
            lanes = slice(v * COLS, (v + 1) * COLS)
            term = dot(at[hp, c], cot[:, lanes]) + dot(at[hp, oc], cot_sib[:, lanes])
            term = term.reshape(NX, QUARTER, COLS)
            gf[hp, v] = term
            gb[hp, v] = term.astype(BF)

    def g1_copy(hp, y_first, d):
        if y_first:
            to = plus(y, d, NY)
            src, device = gb.at[hp, to], dev(to, c, z, x)
        else:
            to = plus(x, d, NX)
            src, device = gb.at[hp, :, to], dev(y, c, z, to)
        return rcopy(src, r1.at[hp, d - 1], g1_send.at[hp, d - 1], g1_recv.at[hp, d - 1], device)

    def g2_copy(hp, y_first, d):
        if y_first:
            to = plus(x, d, NX)
            device = dev(y, c, z, to)
        else:
            to = plus(y, d, NY)
            device = dev(to, c, z, x)
        return rcopy(s1b.at[hp, to], r2.at[hp, d - 1], g2_send.at[hp, d - 1], g2_recv.at[hp, d - 1], device)

    def g3_copy(hp, core):
        return rcopy(
            s2b.at[hp], r3.at[z], g3_send.at[hp, core], g3_recv.at[z], dev(y, core, 4 * c + hp, x)
        )

    def g3_local(hp):
        return pltpu.make_async_copy(s2b.at[hp], r3.at[z], g3_recv.at[z])

    def sum_first(hp, y_first):
        for d in range(3):
            wait_for(r1.at[hp, d], g1_recv.at[hp, d])
        total = gf[hp, y] if y_first else gf[hp, :, x]
        for d in range(3):
            total = total + r1[hp, d].astype(F32)
        s1f[hp] = total
        s1b[hp] = total.astype(BF)
        for d in range(1, 4):
            g2_copy(hp, y_first, d).start()

    def sum_second(hp, y_first):
        for d in range(3):
            wait_for(r2.at[hp, d], g2_recv.at[hp, d])
        total = s1f[hp, x] if y_first else s1f[hp, y]
        for d in range(3):
            total = total + r2[hp, d].astype(F32)
        s2b[hp] = total.astype(BF)
        for core in range(2):
            own = (4 * c + hp == z) & (c == core)
            pl.when(own)(lambda: g3_local(hp).start())
            pl.when(jnp.logical_not(own))(lambda: g3_copy(hp, core).start())

    def heads(i, _):
        for odd in range(2):
            hp = 2 * i + odd
            y_first = odd == 0
            keys_values(hp, 0)
            attend(hp)
            at_copy(hp).start()
            grad(hp)
            for d in range(1, 4):
                g1_copy(hp, y_first, d).start()
            pl.when(hp >= 1)(lambda: sum_first(hp - 1, not y_first))
            pl.when(hp >= 2)(lambda: sum_second(hp - 2, y_first))
        return 0

    lax.fori_loop(0, PAIRS // 2, heads, 0)

    wo_copy.wait()
    small_eye = identity(ROWS)

    def project(part):
        total = None
        for hp in range(PAIRS):
            if part == 0:
                rows, core = at[hp, c], c
            else:
                rows, core = at_sib[hp], oc
            turned = dot_nt(small_eye, rows).astype(BF)
            start = pl.multiple_of(core * (PAIRS * UNIT) + hp * UNIT, UNIT)
            term = dot(turned, w_o_v[pl.ds(start, UNIT), :])
            total = term if total is None else total + term
        return total

    ext[0:ROWS] = project(0)
    sum_first(PAIRS - 1, False)
    sum_second(PAIRS - 2, True)
    for hp in range(PAIRS):
        wait_for(at_sib.at[hp], at_recv.at[hp])
    mixed[...] = (ext[0:ROWS] + project(1)).astype(BF)
    sum_second(PAIRS - 1, False)

    for v in range(NZ):
        wait_for(r3.at[v], g3_recv.at[v])
    total = r3[0].astype(F32)
    for v in range(1, NZ):
        total = total + r3[v].astype(F32)
    wgrad[...] = jnp.where(c == 0, total[:, :UNIT], total[:, UNIT:])

    up.wait_send()
    down.wait_send()
    lohi_copy.wait_send()
    cot_copy.wait_send()

    def sent_own(jj, _):
        j, idx, core = owned(jj)
        for d in (1, 3, 2):
            to_y(jj, d, 0).wait_send()

        @pl.when(idx < DIRECT)
        def _():
            for e in range(1, 4):
                for d in (1, 3, 2):
                    to_y(jj, d, e).wait_send()

        @pl.when(core != c)
        def _():
            for e in range(4):
                to_sibling(jj, e).wait_send()

        return 0

    lax.fori_loop(0, 3, sent_own, 0)
    for r in range(ROWS // CHUNK):
        act_copy(0, r).wait_send()
        act_copy(1, r).wait_send()
        act_pass(r).wait_send()

    def sent_parts(hp, _):
        for t in range(3):
            idx, need = foreign(hp, t)

            @pl.when(need)
            def _(idx=idx):
                for i in range(3):
                    pass_copy(idx, i).wait_send()

        at_copy(hp).wait_send()
        return 0

    lax.fori_loop(0, PAIRS, sent_parts, 0)
    for hp in range(PAIRS):
        for d in range(1, 4):
            g1_copy(hp, hp % 2 == 0, d).wait_send()
            g2_copy(hp, hp % 2 == 0, d).wait_send()
        for core in range(2):
            own = (4 * c + hp == z) & (c == core)
            pl.when(jnp.logical_not(own))(lambda: g3_copy(hp, core).wait_send())


def local(frames, seg, look_back, w_dw, w_qkv, w_o, cotangent):
    me = lax.axis_index("tm")
    row = jnp.pad(seg[0], (ROWS, HALF), constant_values=-1)
    row = lax.dynamic_slice_in_dim(row, me * ROWS, 2 * ROWS + HALF, 0)
    own = row[ROWS : 2 * ROWS]
    same = [
        (row[ROWS - HALF + o : 2 * ROWS - HALF + o] == own).astype(F32) for o in range(KER)
    ]
    cmask = jnp.stack(same + [jnp.zeros_like(same[0])] * 3, 1)
    pair = row[: 2 * ROWS]
    look = lax.dynamic_slice_in_dim(look_back[0], me, 1, 0)
    low = jnp.sum((pair[:, None] < own[None, :]).astype(jnp.int32), 0)
    high = jnp.sum((pair[:, None] <= own[None, :]).astype(jnp.int32), 0)
    low = jnp.maximum(low, jnp.where(look == 1, 0, ROWS))
    lohi = jnp.stack([low, high] + [jnp.zeros_like(low)] * 6, 0)
    vmem, hbm = pl.BlockSpec(memory_space=pltpu.VMEM), pl.BlockSpec(memory_space=pl.ANY)
    dma = pltpu.SemaphoreType.DMA
    return pl.pallas_call(
        kernel,
        name="block",
        out_shape=(
            jax.ShapeDtypeStruct((ROWS, WIDTH), BF),
            jax.ShapeDtypeStruct((QUARTER, UNIT), F32),
        ),
        in_specs=[vmem, vmem, vmem, vmem, vmem, vmem, hbm],
        out_specs=(vmem, vmem),
        scratch_shapes=[
            pltpu.VMEM((3, UNIT, WIDTH), BF),
            pltpu.VMEM((3 * PAIRS, 4, QUARTER, WIDTH), BF),
            pltpu.VMEM((ROWS + 2 * EDGE, WIDTH), F32),
            pltpu.VMEM((2, EDGE, WIDTH), BF),
            pltpu.VMEM((KER, ROWS, 128), F32),
            pltpu.VMEM((4, ROWS, WIDTH), BF),
            pltpu.VMEM((2, 8, ROWS), jnp.int32),
            pltpu.VMEM((WIDTH, WIDTH), BF),
            pltpu.VMEM((ROWS, WIDTH), BF),
            pltpu.VMEM((PAIRS, 2, UNIT, ROWS), BF),
            pltpu.VMEM((PAIRS, 2, 2 * ROWS, UNIT), BF),
            pltpu.VMEM((PAIRS, 2, UNIT, 2 * ROWS), BF),
            pltpu.VMEM((PAIRS, 2, UNIT, ROWS), BF),
            pltpu.VMEM((PAIRS, UNIT, ROWS), BF),
            pltpu.VMEM((PAIRS, NY, NX, QUARTER, COLS), F32),
            pltpu.VMEM((PAIRS, NY, NX, QUARTER, COLS), BF),
            pltpu.VMEM((PAIRS, 3, 4, QUARTER, COLS), BF),
            pltpu.VMEM((PAIRS, 4, QUARTER, COLS), F32),
            pltpu.VMEM((PAIRS, 4, QUARTER, COLS), BF),
            pltpu.VMEM((PAIRS, 3, QUARTER, COLS), BF),
            pltpu.VMEM((PAIRS, QUARTER, COLS), BF),
            pltpu.VMEM((NZ, QUARTER, COLS), BF),
            dma((3, 4, 4)),
            dma((3 * PAIRS, 4)),
            dma((3 * PAIRS, 3)),
            dma((2,)),
            dma((2,)),
            dma((3, 4)),
            dma((3, 4)),
            dma((2,)),
            dma((2,)),
            dma((PAIRS,)),
            dma((PAIRS,)),
            dma((PAIRS, 3)),
            dma((PAIRS, 3)),
            dma((PAIRS, 3)),
            dma((PAIRS, 3)),
            dma((PAIRS, 2)),
            dma((NZ,)),
            dma,
        ],
        compiler_params=pltpu.CompilerParams(
            collective_id=0, has_side_effects=True, vmem_limit_bytes=58 * 2**20
        ),
        cost_estimate=pl.CostEstimate(flops=10**10, bytes_accessed=10**7, transcendentals=2 * 10**6),
    )(frames, cmask, lohi, w_dw, w_qkv, cotangent, w_o)


def solution(mesh):
    placed = (
        P(("dp", "tm"), None),
        P("dp", None),
        P("dp", None),
        P(),
        P(None, "dp"),
        P(),
        P(("dp", "tm"), None),
    )
    return jax.shard_map(
        local,
        mesh=mesh,
        in_specs=placed,
        out_specs=(P(("dp", "tm"), None), P("tm", "dp")),
        check_vma=False,
    )
```

time: 420 us -> 126 us (0.30); the launches traced: 412 us -> 126 us
  waiting for transfers between devices: 324 us -> 0 us
  Pallas kernels: 0 us -> 113 us
  matrix products: 32.8 us -> 0 us
  other arithmetic: 15.8 us -> 2.18 us
  between operations: 13.9 us -> 1.32 us
  starting transfers between devices: 11.6 us -> 0 us
    unnamed x4 -> x0, waiting for transfers between devices: 207 us -> none
    pallas_call x0 -> x1, Pallas kernels: none -> 113 us  [local(): pl.pallas_call(kernel, name='block', out_shape=(jax.ShapeDtypeStruct((ROW...]
    reduce_scatter x1 -> x0, waiting for transfers between devices: 59.6 us -> none  [local(): lax.psum_scatter(grad_term, 'dp', scatter_dimension=1, tiled=True)]
    all_gather x1 -> x0, waiting for transfers between devices: 52.1 us -> none  [local(): weights = lax.all_gather(w_qkv, 'dp', axis=1, tiled=True)]
    dot_general x6 -> x0, matrix products: 32.8 us -> none  [the longest x1 9.13 us: local(): jnp.dot(activ[rows:], weights, preferred_element_type=jnp.float32)]
    ppermute x3 -> x0, starting transfers between devices: 11.4 us -> none  [the longest x1 4.36 us: local(): lax.ppermute(frames[-HALF:], 'tm', [(i, i + 2) for i in range(count - 2)])]
    ppermute x3 -> x0, waiting for transfers between devices: 6.26 us -> none  [the longest x1 6.25 us: local(): before = lax.ppermute(frames, 'tm', [(i, i + 1) for i in range(count - 1)])]
    sub x1 -> x0, other arithmetic: 6.01 us -> none  [local(): raw = jnp.exp(scores - jnp.max(scores, axis=-1, keepdims=True))]
  transfers between devices with their start and end apart: 6 -> 0, of which waited for: 4 -> 0; matrix products, arithmetic and copies ran while one was open for 4% -> 0% of each run, Pallas kernels for 0% -> 0%
where the time goes in v2:
time: 126 us
  Pallas kernels  113 us (90%)
  local copies, waits for them, and re-layouts  9.16 us (7%)
  other arithmetic  2.18 us (2%)
  between operations  1.32 us (1%)
    pallas_call x1, Pallas kernels, local(): pl.pallas_call(kernel, name='block', out_shape=(jax.ShapeDtypeStruct((ROW...  113 us
    unnamed x3, local copies, waits for them, and re-layouts  7.39 us

profile of v2, /device:TPU:97, one launch (start us, length us, event | category | flops | bytes accessed | tf_op | source)
XLA Modules:
  0.0 125.8 jit_solution(9572123449278950492)
XLA Ops:
  0.6 1.2 fusion
  2.5 0.1 pad.7.clone
  2.6 0.1 pad.8.clone
  2.7 0.8 pad_dynamic-slice_fusion
  3.5 0.2 convert_reduce_fusion.1
  3.7 0.1 compare_convert_fusion
  3.8 0.7 add_add_fusion.lohi
  4.5 0.8 copy.17.cmask
  5.3 3.9 %copy.18.w_qkv = bf16[1536,576]{1,0:T(8,128)(2,1)} copy(bf16[1536,576]{0,1:T(8,128)(2,1)} %param.11) | data formatting | bytes 3538944 | tf_op args[4]
  9.2 113.1 %block.1 = (bf16[256,1536]{1,0:T(8,128)(2,1)}, f32[48,192]{1,0:T(8,128)}) custom-call(bf16[256,1536]{1,0:T(8,128)(2,1)} %frames.1, f32[256,8]{1,0:T(8,128)} %copy.17.cmask, s32[8,256]{1,0:T(8,128)} %add_add_fusion.lohi, f32[5,1536]{1,0:T(8,128)} %w_dw.1, bf16[1536,576]{1,0:T(8,128)(2,1)} %copy.18.w_qkv, bf16[256,1536]{1,0:T(8,128)(2,1)} %cot.1, ...), custom_call_target="tpu_custom_call" | custom-call | flops 10000000000 | bytes 10000000 | tf_op jit(solution)/shard_map/block/pallas_call | solution.py:497
  122.3 2.1 %copy.21 = bf16[256,1536]{1,0:T(8,128)(2,1)} copy(bf16[256,1536]{1,0:T(8,128)(2,1)} %get-tuple-element.10) | data formatting | bytes 1572864
  124.4 1.4 %copy.22 = f32[48,192]{1,0:T(8,128)} copy(f32[48,192]{1,0:T(8,128)} %get-tuple-element.11) | data formatting | bytes 73728
  (9 shorter events, 0.1 us)

commit v3 on v2

v3 whole, which is shorter than its diff:
```python
import functools
import math

import jax
import jax.numpy as jnp
from jax import lax
from jax.experimental import pallas as pl
from jax.experimental.pallas import tpu as pltpu
from jax.sharding import PartitionSpec as P

MESH = pl.DeviceIdType.MESH
BF = jnp.bfloat16
F32 = jnp.float32

KER = 5
HALF = 2
ROWS = 256
WIDTH = 1536
HDIM = 96
UNIT = 192
QUARTER = 48
PAIRS = 4
NX, NY, NZ = 4, 4, 8
COLS = 384
SPLIT = 256
BUSY = 3
EDGE = 16
CHUNK = 64
NT = (((1,), (1,)), ((), ()))


def dot(a, b):
    return jnp.dot(a, b, preferred_element_type=F32)


def dot_nt(a, b):
    return lax.dot_general(a, b, NT, preferred_element_type=F32)


def wait_for(ref, sem):
    pltpu.make_async_copy(ref, ref, sem).wait()


def identity(n):
    return (
        lax.broadcasted_iota(jnp.int32, (n, n), 0) == lax.broadcasted_iota(jnp.int32, (n, n), 1)
    ).astype(BF)


def kernel(
    frames, seg, look, w_dw, wt, cot, w_o, mixed, wgrad,
    units, ext, halo, seg_b, mask_b, acts, lohi_b, w_o_v, cot_sib, q_t, k_n, v_t, at, at_sib,
    gf_a, gf_b, gb_a, gb_b, r1_a, r1_b, s1f_a, s1f_b, s1b_a, s1b_b, r2_a, r2_b, s2b, r3,
    w_send, w_recv, f_send, halo_send, halo_recv, act_send, act_recv, small_send, small_recv,
    at_send, at_recv, g1_send, g1_recv, g2_send, g2_recv, g3_send, g3_recv, wo_sem,
):
    dp, tm = lax.axis_index("dp"), lax.axis_index("tm")
    y, c = lax.div(dp, 2), lax.rem(dp, 2)
    z, x = lax.div(tm, 4), lax.rem(tm, 4)
    oc = 1 - c

    def dev(yy, cc, zz, xx):
        return {"dp": yy * 2 + cc, "tm": zz * 4 + xx}

    def plus(v, d, n):
        return lax.rem(v + d, n)

    def rcopy(src, dst, send, recv, device):
        return pltpu.make_async_remote_copy(
            src_ref=src, dst_ref=dst, send_sem=send, recv_sem=recv,
            device_id=device, device_id_type=MESH,
        )

    sibling = dev(y, oc, z, x)
    following = {"dp": dp, "tm": plus(tm, 1, 32)}
    preceding = {"dp": dp, "tm": plus(tm, 31, 32)}
    x_low = dev(y, c, z, plus(x, NX - 1, NX))

    partners = [sibling, following, preceding]
    for d in range(1, NY):
        partners += [dev(plus(y, d, NY), c, z, x), dev(plus(y, d, NY), oc, z, x)]
    for d in range(1, NX):
        partners += [dev(y, c, z, plus(x, d, NX))]
    for d in range(1, NZ):
        partners += [dev(y, c, plus(z, d, NZ), x), dev(y, oc, plus(z, d, NZ), x)]
    barrier = pltpu.get_barrier_semaphore()
    for device in partners:
        pl.semaphore_signal(barrier, inc=1, device_id=device, device_id_type=MESH)

    wo_copy = pltpu.make_async_copy(w_o, w_o_v, wo_sem)
    wo_copy.start()

    def seg_of(stretch, there):
        inside = jnp.clip(stretch, 0, 31)
        row = seg[:, pl.ds(pl.multiple_of(inside * ROWS, ROWS), ROWS)]
        return jnp.where(there, row, -1)

    seg_rows = [seg_of(tm - 1, tm > 0), seg_of(tm, tm >= 0), seg_of(tm + 1, tm < 31)]
    seg_cols = [jnp.transpose(jnp.broadcast_to(row, (128, ROWS))) for row in seg_rows]
    seg_b[0:EDGE] = seg_cols[0][ROWS - EDGE :]
    seg_b[EDGE : EDGE + ROWS] = seg_cols[1]
    seg_b[EDGE + ROWS :] = seg_cols[2][:EDGE]
    for o in range(KER):
        same = seg_b[EDGE - HALF + o : EDGE - HALF + o + ROWS] == seg_cols[1]
        mask_b[o] = jnp.where(same, 1.0, 0.0)
    looks = jnp.sum(
        jnp.where(lax.broadcasted_iota(jnp.int32, (1, 32), 1) == tm, look[...], 0), axis=1, keepdims=True
    )
    pair = jnp.concatenate([seg_cols[0], seg_cols[1]], 0)
    pair = jnp.concatenate([pair, pair], 1)
    low = jnp.sum(jnp.where(pair < seg_rows[1], 1, 0), axis=0, keepdims=True)
    high = jnp.sum(jnp.where(pair <= seg_rows[1], 1, 0), axis=0, keepdims=True)
    low = jnp.maximum(low, jnp.where(looks == 1, 0, ROWS))
    lohi_b[c, 0:1] = low
    lohi_b[c, 1:2] = high
    ext[EDGE : EDGE + ROWS] = frames[...].astype(F32)

    pl.semaphore_wait(barrier, len(partners))

    up = rcopy(frames.at[ROWS - EDGE : ROWS], halo.at[0], halo_send.at[0], halo_recv.at[0], following)
    down = rcopy(frames.at[0:EDGE], halo.at[1], halo_send.at[1], halo_recv.at[1], preceding)
    up.start()
    down.start()
    lohi_copy = rcopy(lohi_b.at[c], lohi_b.at[c], small_send.at[0], small_recv.at[0], sibling)
    lohi_copy.start()

    mine = lax.rem(x, 2) + 2 * lax.rem(z, 2)
    from_x = (1 - lax.rem(x, 2)) + 2 * lax.rem(z, 2)
    from_z = lax.rem(x, 2) + 2 * (1 - lax.rem(z, 2))
    from_xz = (1 - lax.rem(x, 2)) + 2 * (1 - lax.rem(z, 2))

    def owned(j):
        u = 3 * dp + j
        return lax.rem(u, 4), lax.div(u, 8), lax.rem(lax.div(u, 4), 2)

    def to_y(j, d):
        hp, t, core = owned(j)
        idx = hp * 3 + t
        return rcopy(
            wt.at[pl.ds(pl.multiple_of(j * UNIT + mine * QUARTER, QUARTER), QUARTER)],
            units.at[idx, mine], w_send.at[j, d], w_recv.at[idx, mine], dev(plus(y, d, NY), core, z, x),
        )

    def to_sibling(j, e):
        hp, t, core = owned(j)
        idx = hp * 3 + t
        return rcopy(
            wt.at[j * UNIT + e * QUARTER : j * UNIT + (e + 1) * QUARTER],
            units.at[idx, e], w_send.at[j, 4 + e], w_recv.at[idx, e], sibling,
        )

    def send_own(g):
        for j in range(3):
            hp, t, core = owned(j)
            idx = hp * 3 + t

            @pl.when(hp == g)
            def _(j=j):
                for d in (2, 1, 3):
                    to_y(j, d).start()

            @pl.when((hp == g) & (core != c))
            def _(j=j):
                for e in range(4):
                    to_sibling(j, e).start()

            @pl.when((hp == g) & (core == c))
            def _(j=j, idx=idx):
                for e in range(4):
                    pltpu.make_async_copy(
                        wt.at[j * UNIT + e * QUARTER : j * UNIT + (e + 1) * QUARTER],
                        units.at[idx, e], w_recv.at[idx, e],
                    ).start()

    send_own(0)
    send_own(1)

    wait_for(halo.at[0], halo_recv.at[0])
    wait_for(halo.at[1], halo_recv.at[1])
    ext[0:EDGE] = halo[0].astype(F32)
    ext[EDGE + ROWS :] = halo[1].astype(F32)

    def act_copy(i, r):
        rows = pl.ds(r * CHUNK, CHUNK)
        device, place = ((sibling, 2 * c + 1), (following, 2 * c))[i]
        return rcopy(
            acts.at[2 * c + 1, rows], acts.at[place, rows], act_send.at[i, r], act_recv.at[i, r], device
        )

    def act_pass(r):
        rows = pl.ds(r * CHUNK, CHUNK)
        return rcopy(
            acts.at[2 * c, rows], acts.at[2 * c, rows], act_send.at[2, r], act_recv.at[2, r], sibling
        )

    for r in range(ROWS // CHUNK):

        def column(i, _, r=r):
            lanes = pl.ds(pl.multiple_of(i * 128, 128), 128)
            total = jnp.zeros((CHUNK, 128), F32)
            for o in range(KER):
                window = ext[EDGE - HALF + r * CHUNK + o : EDGE - HALF + r * CHUNK + o + CHUNK, lanes]
                total = total + w_dw[o : o + 1, lanes] * window * mask_b[o, r * CHUNK : (r + 1) * CHUNK]
            acts[2 * c + 1, r * CHUNK : (r + 1) * CHUNK, lanes] = (total / (1.0 + jnp.exp(-total))).astype(BF)
            return 0

        lax.fori_loop(0, WIDTH // 128, column, 0)
        act_copy(1, r).start()
        act_copy(0, r).start()

    cot_copy = rcopy(cot, cot_sib, small_send.at[1], small_recv.at[1], sibling)
    cot_copy.start()

    def foreign(hp, t):
        u = 8 * t + 4 * c + hp
        idx = hp * 3 + t
        return idx, lax.div(u, 6) != y

    def along_z(idx):
        even = lax.rem(idx, 2) == 0
        third = lax.rem(lax.div(idx, 3) + lax.rem(idx, 3), 3) == 0
        step = jnp.where(jnp.where(x == BUSY, third, even), 1, NZ - 1)
        return dev(y, c, plus(z, step, NZ), x)

    def pass_copy(idx, t, i):
        part = (mine, mine, from_z if t == 2 else from_x)[i]
        late = dev(y, c, z, plus(x, jnp.where(idx >= 6, 1, NX - 1), NX))
        if i == 0:
            device = late if t == 0 else x_low
        elif i == 2 and t == 2:
            device = late
        else:
            device = along_z(idx)
        return rcopy(units.at[idx, part], units.at[idx, part], f_send.at[idx, i], w_recv.at[idx, part], device)

    def pump_first(hp):
        for t in range(3):
            idx, need = foreign(hp, t)

            @pl.when(need)
            def _(idx=idx, t=t):
                wait_for(units.at[idx, mine], w_recv.at[idx, mine])
                pass_copy(idx, t, 0).start()
                pass_copy(idx, t, 1).start()

    def pump_second(hp):
        for t in range(3):
            idx, need = foreign(hp, t)

            @pl.when(need)
            def _(idx=idx, t=t):
                arrived = from_z if t == 2 else from_x
                wait_for(units.at[idx, arrived], w_recv.at[idx, arrived])
                pass_copy(idx, t, 2).start()

    def wait_unit(hp, t):
        idx, need = foreign(hp, t)

        @pl.when(need)
        def _():
            other = from_x if t == 2 else from_z
            wait_for(units.at[idx, other], w_recv.at[idx, other])
            wait_for(units.at[idx, from_xz], w_recv.at[idx, from_xz])

        @pl.when(jnp.logical_not(need))
        def _():
            for e in range(4):
                wait_for(units.at[idx, e], w_recv.at[idx, e])

    def unit(hp, t):
        return units[hp * 3 + t].reshape(UNIT, WIDTH)

    def keys_values(hp, part):
        where = slice(part * ROWS, (part + 1) * ROWS)
        for s in range(2):
            k_n[hp, s, where] = dot_nt(acts[2 * s + part], unit(hp, 1)).astype(BF)
            v_t[hp, s, :, where] = dot_nt(unit(hp, 2), acts[2 * s + part]).astype(BF)

    def own_part(hp):
        for t in range(3):
            wait_unit(hp, t)
        for s in range(2):
            q_t[hp, s] = dot_nt(unit(hp, 0), acts[2 * s + 1]).astype(BF)
        keys_values(hp, 1)

    factor = math.log2(math.e) / math.sqrt(HDIM)

    def attend(hp):
        def one(s, _):
            q = q_t[hp, s]
            zero = jnp.zeros((HDIM, ROWS), BF)
            both = jnp.concatenate(
                [jnp.concatenate([q[:HDIM], zero], 0), jnp.concatenate([zero, q[HDIM:]], 0)], 1
            )
            scores = dot(k_n[hp, s], both)
            bounds = lohi_b[s]
            at_j = lax.broadcasted_iota(jnp.int32, (2 * ROWS, ROWS), 0)
            allowed = (at_j >= bounds[0:1]) & (at_j < bounds[1:2])
            for e in range(2):
                mine_scores = jnp.where(allowed, scores[:, e * ROWS : (e + 1) * ROWS], -1e30)
                top = jnp.max(mine_scores, axis=0, keepdims=True)
                raw = jnp.exp2((mine_scores - top) * factor)
                probs = (raw * (1.0 / jnp.sum(raw, axis=0, keepdims=True))).astype(BF)
                at[hp, s, e * HDIM : (e + 1) * HDIM] = dot(
                    v_t[hp, s, e * HDIM : (e + 1) * HDIM], probs
                ).astype(BF)
            return 0

        lax.fori_loop(0, 2, one, 0)

    def at_copy(hp):
        return rcopy(at.at[hp, oc], at_sib.at[hp], at_send.at[hp], at_recv.at[hp], sibling)

    def grad(hp):
        for v in range(NY):
            lanes = slice(v * COLS, (v + 1) * COLS)
            term = dot(at[hp, c], cot[:, lanes]) + dot(at[hp, oc], cot_sib[:, lanes])
            term = term.reshape(NX, QUARTER, COLS)

            def keep(wide_y):
                for i, lanes in enumerate((slice(0, SPLIT), slice(SPLIT, COLS))):
                    part = term[:, :, lanes]
                    if wide_y == (i == 0):
                        (gf_a, gf_b)[i][hp, v] = part
                        (gb_a, gb_b)[i][hp, v] = part.astype(BF)
                    else:
                        (gf_a, gf_b)[i][hp, :, v] = part
                        (gb_a, gb_b)[i][hp, :, v] = part.astype(BF)

            pl.when(lax.rem(hp, 2) == 0)(lambda keep=keep: keep(True))
            pl.when(lax.rem(hp, 2) == 1)(lambda keep=keep: keep(False))

    def along_y(hp, i, stage):
        return lax.rem(hp + i + stage, 2) == 0

    def toward(on_y, d):
        ty, tx = plus(y, d, NY), plus(x, d, NX)
        device = {"dp": jnp.where(on_y, ty * 2 + c, dp), "tm": jnp.where(on_y, tm, z * 4 + tx)}
        return jnp.where(on_y, ty, tx), device

    def own_place(on_y):
        return jnp.where(on_y, y, x)

    def g1_copy(hp, i, d):
        to, device = toward(along_y(hp, i, 0), d)
        return rcopy(
            (gb_a, gb_b)[i].at[hp, to], (r1_a, r1_b)[i].at[hp, d - 1],
            g1_send.at[hp, i, d - 1], g1_recv.at[hp, i, d - 1], device,
        )

    def g2_copy(hp, i, d):
        to, device = toward(along_y(hp, i, 1), d)
        return rcopy(
            (s1b_a, s1b_b)[i].at[hp, to], (r2_a, r2_b)[i].at[hp, d - 1],
            g2_send.at[hp, i, d - 1], g2_recv.at[hp, i, d - 1], device,
        )

    def g3_copy(hp, core):
        return rcopy(
            s2b.at[hp], r3.at[z], g3_send.at[hp, core], g3_recv.at[z], dev(y, core, 4 * c + hp, x)
        )

    def g3_local(hp):
        return pltpu.make_async_copy(s2b.at[hp], r3.at[z], g3_recv.at[z])

    def send_grad(hp):
        for d in (2, 1, 3):
            for i in range(2):
                g1_copy(hp, i, d).start()

    def sum_first(hp):
        for i in range(2):
            arrived, own = (r1_a, r1_b)[i], (gf_a, gf_b)[i]
            total = own[hp, own_place(along_y(hp, i, 0))]
            for d in (1, 3, 2):
                wait_for(arrived.at[hp, d - 1], g1_recv.at[hp, i, d - 1])
                total = total + arrived[hp, d - 1].astype(F32)
            (s1f_a, s1f_b)[i][hp] = total
            (s1b_a, s1b_b)[i][hp] = total.astype(BF)
            for d in (2, 1, 3):
                g2_copy(hp, i, d).start()

    def sum_second(hp):
        totals = []
        for i in range(2):
            arrived = (r2_a, r2_b)[i]
            total = (s1f_a, s1f_b)[i][hp, own_place(along_y(hp, i, 1))]
            for d in (1, 3, 2):
                wait_for(arrived.at[hp, d - 1], g2_recv.at[hp, i, d - 1])
                total = total + arrived[hp, d - 1].astype(F32)
            totals.append(total.astype(BF))
        s2b[hp] = jnp.concatenate(totals, 1)
        for core in range(2):
            own = (4 * c + hp == z) & (c == core)
            pl.when(own)(lambda: g3_local(hp).start())
            pl.when(jnp.logical_not(own))(lambda: g3_copy(hp, core).start())

    def chunks(act):
        for r in range(ROWS // CHUNK):
            act(r, pl.ds(r * CHUNK, CHUNK))

    def both_heads(hp):
        keys_values(hp, 0)
        attend(hp)
        at_copy(hp).start()
        grad(hp)
        send_grad(hp)

    def slot(g, _):
        pl.when(g < PAIRS - 1)(lambda: send_own(g + 1))
        pl.when(g < PAIRS + 1)(lambda: pump_first(g - 1))
        pl.when((g >= 2) & (g < PAIRS + 2))(lambda: pump_second(g - 2))

        @pl.when(g == 3)
        def _():
            chunks(lambda r, rows: wait_for(acts.at[2 * oc + 1, rows], act_recv.at[0, r]))

        pl.when((g >= 3) & (g <= 5))(lambda: own_part(g - 3))

        @pl.when(g == 4)
        def _():
            def onward(r, rows):
                wait_for(acts.at[2 * c, rows], act_recv.at[1, r])
                act_pass(r).start()

            chunks(onward)
            chunks(lambda r, rows: wait_for(acts.at[2 * oc, rows], act_recv.at[2, r]))
            wait_for(lohi_b.at[oc], small_recv.at[0])
            wait_for(cot_sib, small_recv.at[1])

        pl.when(g >= 4)(lambda: both_heads(g - 4))
        pl.when(g >= 6)(lambda: sum_first(g - 6))
        pl.when(g >= 7)(lambda: sum_second(g - 7))
        pl.when(g == 6)(lambda: own_part(PAIRS - 1))
        return 0

    lax.fori_loop(1, PAIRS + 4, slot, 0)

    wo_copy.wait()
    small_eye = identity(ROWS)

    def project(part):
        total = None
        for hp in range(PAIRS):
            if part == 0:
                rows, core = at[hp, c], c
            else:
                rows, core = at_sib[hp], oc
            turned = dot_nt(small_eye, rows).astype(BF)
            start = pl.multiple_of(core * (PAIRS * UNIT) + hp * UNIT, UNIT)
            term = dot(turned, w_o_v[pl.ds(start, UNIT), :])
            total = term if total is None else total + term
        return total

    ext[0:ROWS] = project(0)
    sum_first(PAIRS - 2)
    sum_second(PAIRS - 3)
    sum_first(PAIRS - 1)
    sum_second(PAIRS - 2)
    for hp in range(PAIRS):
        wait_for(at_sib.at[hp], at_recv.at[hp])
    mixed[...] = (ext[0:ROWS] + project(1)).astype(BF)
    sum_second(PAIRS - 1)

    for v in range(NZ):
        wait_for(r3.at[v], g3_recv.at[v])
    total = r3[0].astype(F32)
    for v in range(1, NZ):
        total = total + r3[v].astype(F32)
    wgrad[...] = jnp.where(c == 0, total[:, :UNIT], total[:, UNIT:])

    up.wait_send()
    down.wait_send()
    lohi_copy.wait_send()
    cot_copy.wait_send()

    for j in range(3):
        for d in (2, 1, 3):
            to_y(j, d).wait_send()

        @pl.when(owned(j)[2] != c)
        def _(j=j):
            for e in range(4):
                to_sibling(j, e).wait_send()

    for r in range(ROWS // CHUNK):
        act_copy(0, r).wait_send()
        act_copy(1, r).wait_send()
        act_pass(r).wait_send()

    def sent_parts(hp, _):
        for t in range(3):
            idx, need = foreign(hp, t)

            @pl.when(need)
            def _(idx=idx, t=t):
                for i in range(3):
                    pass_copy(idx, t, i).wait_send()

        at_copy(hp).wait_send()
        return 0

    lax.fori_loop(0, PAIRS, sent_parts, 0)
    for hp in range(PAIRS):
        for i in range(2):
            for d in range(1, 4):
                g1_copy(hp, i, d).wait_send()
                g2_copy(hp, i, d).wait_send()
        for core in range(2):
            own = (4 * c + hp == z) & (c == core)
            pl.when(jnp.logical_not(own))(lambda: g3_copy(hp, core).wait_send())


def local(frames, seg, look_back, w_dw, w_qkv, w_o, cotangent):
    vmem, hbm = pl.BlockSpec(memory_space=pltpu.VMEM), pl.BlockSpec(memory_space=pl.ANY)
    dma = pltpu.SemaphoreType.DMA
    return pl.pallas_call(
        kernel,
        name="block",
        out_shape=(
            jax.ShapeDtypeStruct((ROWS, WIDTH), BF),
            jax.ShapeDtypeStruct((QUARTER, UNIT), F32),
        ),
        in_specs=[vmem, vmem, vmem, vmem, vmem, vmem, hbm],
        out_specs=(vmem, vmem),
        scratch_shapes=[
            pltpu.VMEM((3 * PAIRS, 4, QUARTER, WIDTH), BF),
            pltpu.VMEM((ROWS + 2 * EDGE, WIDTH), F32),
            pltpu.VMEM((2, EDGE, WIDTH), BF),
            pltpu.VMEM((ROWS + 2 * EDGE, 128), jnp.int32),
            pltpu.VMEM((KER, ROWS, 128), F32),
            pltpu.VMEM((4, ROWS, WIDTH), BF),
            pltpu.VMEM((2, 8, ROWS), jnp.int32),
            pltpu.VMEM((WIDTH, WIDTH), BF),
            pltpu.VMEM((ROWS, WIDTH), BF),
            pltpu.VMEM((PAIRS, 2, UNIT, ROWS), BF),
            pltpu.VMEM((PAIRS, 2, 2 * ROWS, UNIT), BF),
            pltpu.VMEM((PAIRS, 2, UNIT, 2 * ROWS), BF),
            pltpu.VMEM((PAIRS, 2, UNIT, ROWS), BF),
            pltpu.VMEM((PAIRS, UNIT, ROWS), BF),
            pltpu.VMEM((PAIRS, 4, 4, QUARTER, SPLIT), F32),
            pltpu.VMEM((PAIRS, 4, 4, QUARTER, COLS - SPLIT), F32),
            pltpu.VMEM((PAIRS, 4, 4, QUARTER, SPLIT), BF),
            pltpu.VMEM((PAIRS, 4, 4, QUARTER, COLS - SPLIT), BF),
            pltpu.VMEM((PAIRS, 3, 4, QUARTER, SPLIT), BF),
            pltpu.VMEM((PAIRS, 3, 4, QUARTER, COLS - SPLIT), BF),
            pltpu.VMEM((PAIRS, 4, QUARTER, SPLIT), F32),
            pltpu.VMEM((PAIRS, 4, QUARTER, COLS - SPLIT), F32),
            pltpu.VMEM((PAIRS, 4, QUARTER, SPLIT), BF),
            pltpu.VMEM((PAIRS, 4, QUARTER, COLS - SPLIT), BF),
            pltpu.VMEM((PAIRS, 3, QUARTER, SPLIT), BF),
            pltpu.VMEM((PAIRS, 3, QUARTER, COLS - SPLIT), BF),
            pltpu.VMEM((PAIRS, QUARTER, COLS), BF),
            pltpu.VMEM((NZ, QUARTER, COLS), BF),
            dma((3, 8)),
            dma((3 * PAIRS, 4)),
            dma((3 * PAIRS, 3)),
            dma((2,)),
            dma((2,)),
            dma((3, 4)),
            dma((3, 4)),
            dma((2,)),
            dma((2,)),
            dma((PAIRS,)),
            dma((PAIRS,)),
            dma((PAIRS, 2, 3)),
            dma((PAIRS, 2, 3)),
            dma((PAIRS, 2, 3)),
            dma((PAIRS, 2, 3)),
            dma((PAIRS, 2)),
            dma((NZ,)),
            dma,
        ],
        compiler_params=pltpu.CompilerParams(
            collective_id=0, has_side_effects=True, vmem_limit_bytes=58 * 2**20
        ),
        cost_estimate=pl.CostEstimate(flops=10**10, bytes_accessed=10**7, transcendentals=2 * 10**6),
    )(frames, seg, look_back, w_dw, w_qkv.T, cotangent, w_o)


def solution(mesh):
    placed = (
        P(("dp", "tm"), None),
        P("dp", None),
        P("dp", None),
        P(),
        P(None, "dp"),
        P(),
        P(("dp", "tm"), None),
    )
    return jax.shard_map(
        local,
        mesh=mesh,
        in_specs=placed,
        out_specs=(P(("dp", "tm"), None), P("tm", "dp")),
        check_vma=False,
    )
```

time: 126 us -> 91.9 us (0.73)
  Pallas kernels: 113 us -> 87.6 us
  local copies, waits for them, and re-layouts: 9.16 us -> 3.48 us
  other arithmetic: 2.18 us -> 0 us
    pallas_call x1, Pallas kernels: 113 us -> 87.6 us  [local(): pl.pallas_call(kernel, name='block', out_shape=(jax.ShapeDtypeStruct((ROW...]
    unnamed x3 -> x2, local copies, waits for them, and re-layouts: 7.39 us -> 3.48 us
where the time goes in v3:
time: 91.9 us; the launch traced here: 91.7 us
  Pallas kernels  87.6 us (95%)
  local copies, waits for them, and re-layouts  3.48 us (4%)
    pallas_call x1, Pallas kernels, local(): pl.pallas_call(kernel, name='block', out_shape=(jax.ShapeDtypeStruct((ROW...  87.6 us
    unnamed x2, local copies, waits for them, and re-layouts  3.48 us

profile of v3, /device:TPU:97, one launch (start us, length us, event | category | flops | bytes accessed | tf_op | source)
XLA Modules:
  0.0 91.7 jit_solution(5599669080177840139)
XLA Ops:
  0.6 87.6 %block.1 = (bf16[256,1536]{1,0:T(8,128)(2,1)}, f32[48,192]{1,0:T(8,128)}) custom-call(bf16[256,1536]{1,0:T(8,128)(2,1)} %frames.1, s32[1,8192]{1,0:T(1,128)} %seg.1, s32[1,32]{1,0:T(1,128)} %look.1, f32[5,1536]{1,0:T(8,128)} %w_dw.1, bf16[576,1536]{1,0:T(8,128)(2,1)} %bitcast.1, bf16[256,1536]{1,0:T(8,128)(2,1)} %cot.1, bf16[1536,1536]{1,0:T(8,128)(2,1)} %w_o.1), custom_call_target="tpu_custom_call" | custom-call | flops 10000000000 | bytes 10000000 | tf_op jit(solution)/shard_map/block/pallas_call | solution.py:517
  88.3 2.1 %copy.11 = bf16[256,1536]{1,0:T(8,128)(2,1)} copy(bf16[256,1536]{1,0:T(8,128)(2,1)} %get-tuple-element.4) | data formatting | bytes 1572864
  90.3 1.4 %copy.12 = f32[48,192]{1,0:T(8,128)} copy(f32[48,192]{1,0:T(8,128)} %get-tuple-element.5) | data formatting | bytes 73728

commit v4 on v3

--- a/solution.py
+++ b/solution.py
@@ -224,7 +224,7 @@
 
     def pass_copy(idx, t, i):
         part = (mine, mine, from_z if t == 2 else from_x)[i]
-        late = dev(y, c, z, plus(x, jnp.where(idx >= 6, 1, NX - 1), NX))
+        late = dev(y, c, z, plus(x, jnp.where(idx >= 3, 1, NX - 1), NX))
         if i == 0:
             device = late if t == 0 else x_low
         elif i == 2 and t == 2:

time: 91.9 us -> 90.9 us (0.989)
  the two profiles are of different devices: /device:TPU:97 before, /device:TPU:1 now
where the time goes in v4:
time: 90.9 us; the launch traced here: 90.7 us
  Pallas kernels  86.5 us (95%)
  local copies, waits for them, and re-layouts  3.48 us (4%)
    pallas_call x1, Pallas kernels, local(): pl.pallas_call(kernel, name='block', out_shape=(jax.ShapeDtypeStruct((ROW...  86.5 us
    unnamed x2, local copies, waits for them, and re-layouts  3.48 us

profile of v4, /device:TPU:1, one launch (start us, length us, event | category | flops | bytes accessed | tf_op | source)
XLA Modules:
  0.0 90.7 jit_solution(8153966217146774264)
XLA Ops:
  0.6 86.5 %block.1 = (bf16[256,1536]{1,0:T(8,128)(2,1)}, f32[48,192]{1,0:T(8,128)}) custom-call(bf16[256,1536]{1,0:T(8,128)(2,1)} %frames.1, s32[1,8192]{1,0:T(1,128)} %seg.1, s32[1,32]{1,0:T(1,128)} %look.1, f32[5,1536]{1,0:T(8,128)} %w_dw.1, bf16[576,1536]{1,0:T(8,128)(2,1)} %bitcast.1, bf16[256,1536]{1,0:T(8,128)(2,1)} %cot.1, bf16[1536,1536]{1,0:T(8,128)(2,1)} %w_o.1), custom_call_target="tpu_custom_call" | custom-call | flops 10000000000 | bytes 10000000 | tf_op jit(solution)/shard_map/block/pallas_call | solution.py:517
  87.2 2.1 %copy.11 = bf16[256,1536]{1,0:T(8,128)(2,1)} copy(bf16[256,1536]{1,0:T(8,128)(2,1)} %get-tuple-element.4) | data formatting | bytes 1572864
  89.2 1.4 %copy.12 = f32[48,192]{1,0:T(8,128)} copy(f32[48,192]{1,0:T(8,128)} %get-tuple-element.5) | data formatting | bytes 73728

commit v5 on v4

--- a/solution.py
+++ b/solution.py
@@ -22,7 +22,7 @@
 PAIRS = 4
 NX, NY, NZ = 4, 4, 8
 COLS = 384
-SPLIT = 256
+SPLIT = 128
 BUSY = 3
 EDGE = 16
 CHUNK = 64

time: 90.9 us -> 91.4 us (level)
  the two profiles are of different devices: /device:TPU:1 before, /device:TPU:97 now
where the time goes in v5:
time: 91.4 us; the launch traced here: 91.2 us
  Pallas kernels  87.1 us (95%)
  local copies, waits for them, and re-layouts  3.48 us (4%)
    pallas_call x1, Pallas kernels, local(): pl.pallas_call(kernel, name='block', out_shape=(jax.ShapeDtypeStruct((ROW...  87.1 us
    unnamed x2, local copies, waits for them, and re-layouts  3.48 us

profile of v5, /device:TPU:97, one launch (start us, length us, event | category | flops | bytes accessed | tf_op | source)
XLA Modules:
  0.0 91.2 jit_solution(10781744613892088528)
XLA Ops:
  0.6 87.1 %block.1 = (bf16[256,1536]{1,0:T(8,128)(2,1)}, f32[48,192]{1,0:T(8,128)}) custom-call(bf16[256,1536]{1,0:T(8,128)(2,1)} %frames.1, s32[1,8192]{1,0:T(1,128)} %seg.1, s32[1,32]{1,0:T(1,128)} %look.1, f32[5,1536]{1,0:T(8,128)} %w_dw.1, bf16[576,1536]{1,0:T(8,128)(2,1)} %bitcast.1, bf16[256,1536]{1,0:T(8,128)(2,1)} %cot.1, bf16[1536,1536]{1,0:T(8,128)(2,1)} %w_o.1), custom_call_target="tpu_custom_call" | custom-call | flops 10000000000 | bytes 10000000 | tf_op jit(solution)/shard_map/block/pallas_call | solution.py:517
  87.7 2.1 %copy.11 = bf16[256,1536]{1,0:T(8,128)(2,1)} copy(bf16[256,1536]{1,0:T(8,128)(2,1)} %get-tuple-element.4) | data formatting | bytes 1572864
  89.8 1.4 %copy.12 = f32[48,192]{1,0:T(8,128)} copy(f32[48,192]{1,0:T(8,128)} %get-tuple-element.5) | data formatting | bytes 73728
